TPU v7x, 32 devices: a whole 2x2x4 slice. The times are simulated.
32 devices in a mesh: fsdp: 4 (over y, x), heads: 4 (over z), tensor: 2 (over core).
Axes of the slice: x: 2, y: 2, z: 4, core: 2. Of those that a mesh axis runs over, the one named last changes fastest.
Arguments:
- tokens: bfloat16 [12608, 512], P(('fsdp', 'heads', 'tensor')), may hold values from -6 to 6
- cotangent: bfloat16 [12608, 512], P(('fsdp', 'heads', 'tensor')), may hold values from -6 to 6
- image_counts: int32 [4], P('fsdp'), may hold values from 15 to 16
- w_qkv: bfloat16 [1, 3, 512, 512], P(None, None, 'fsdp', ('heads', 'tensor')), may hold values from -0.25 to 0.25
- w_out: bfloat16 [1, 512, 512], P(None, ('heads', 'tensor'), 'fsdp'), may hold values from -1 to 1
- ln_gain: float32 [1, 2, 512], replicated, may hold values from 0.5 to 1.5
- ln_bias: float32 [1, 2, 512], replicated, may hold values from -1.75 to 1.75
- w_router: bfloat16 [1, 512, 32], replicated, may hold values from -0.1875 to 0.1875
- w_in: bfloat16 [1, 32, 512, 2048], P(None, 'heads', 'fsdp', 'tensor'), may hold values from -0.25 to 0.25
- w_back: bfloat16 [1, 32, 2048, 512], P(None, 'heads', 'tensor', 'fsdp'), may hold values from -2 to 2
- expert_ids: int32 [1, 12608, 2], P(None, 'fsdp'), may hold values from 0 to 31, as said below
- slots: int32 [1, 12608, 2], P(None, 'fsdp'), may hold values from -1 to 255, as said below
Outputs:
- output: bfloat16 [12608, 512], P(('fsdp', 'heads', 'tensor'))
- tokens_grad: float32 [12608, 512], P(('fsdp', 'heads', 'tensor'))
- w_qkv_grad: float32 [1, 3, 512, 512], P(None, None, 'fsdp', ('heads', 'tensor'))
- w_out_grad: float32 [1, 512, 512], P(None, ('heads', 'tensor'), 'fsdp')
- ln_gain_grad: float32 [1, 2, 512], replicated
- ln_bias_grad: float32 [1, 2, 512], replicated
- w_router_grad: float32 [1, 512, 32], replicated
- w_in_grad: float32 [1, 32, 512, 2048], P(None, 'heads', 'fsdp', 'tensor')
- w_back_grad: float32 [1, 32, 2048, 512], P(None, 'heads', 'tensor', 'fsdp')
Inputs may be any that keep to these rules, and one draw needn't show every extreme that they name: `expert_ids`: each token names two different experts. `slots`: a choice's slot is its place, in token order, among the choices of its group and block that name the same expert, or -1 where that place is 256 or more; in every group and block some expert is named more than 256 times.
All inputs are finite; a program needn't handle non-finite values.
Results may differ from a plain program's by a relative error of at most 0.012.
Values may be sent and summed in bfloat16 or wider, within the bound.
A program may use at most 192 MiB of HBM per device.

v0:
```python
import jax
import jax.numpy as jnp
from jax import lax
from jax.experimental import pallas as pl
from jax.experimental.pallas import tpu as pltpu
from jax.sharding import PartitionSpec as P

HEAD = 64
SEQ = 197
LAYERS = 1
CAP = 256


def layer_norm(value, ln_gains, ln_shift):
    centred = value - jnp.mean(value, axis=-1, keepdims=True)
    spread = jnp.mean(centred * centred, axis=-1, keepdims=True)
    return centred * lax.rsqrt(spread + 1e-06) * ln_gains + ln_shift


def gelu_exact(value):
    return jax.nn.gelu(value, approximate=False)


def with_zero_row(matrix):
    return jnp.concatenate([matrix, jnp.zeros((1,) + matrix.shape[1:], matrix.dtype)], axis=0)


def slot_tables(named_expert, slot_rows, first_expert, local_experts):
    group_rows = named_expert.shape[0]
    is_local = (
        (slot_rows >= 0)
        & (named_expert >= first_expert)
        & (named_expert < first_expert + local_experts)
    )
    places = jnp.where(
        is_local, (named_expert - first_expert) * CAP + slot_rows, local_experts * CAP
    )
    picked = jnp.full((local_experts * CAP + 1,), 2 * group_rows, jnp.int32)
    picked = picked.at[places.reshape(-1)].set(jnp.arange(2 * group_rows, dtype=jnp.int32))
    return (places, picked[: local_experts * CAP])


def joined_qkv(qkv_weight):
    head_cols = qkv_weight.shape[2]
    return jnp.transpose(qkv_weight, (1, 0, 2)).reshape(qkv_weight.shape[1], 3 * head_cols)


def forward_block(
    residual, weights, ln_gains, ln_shift, router_weight, named_expert, slot_rows, first_expert
):
    qkv_weight, out_weight, in_weight, back_weight = weights
    own_rows, widths = residual.shape
    group_rows = named_expert.shape[0]
    head_cols = qkv_weight.shape[2]
    local_experts = in_weight.shape[0]
    head_shape = (group_rows // SEQ, SEQ, head_cols // HEAD, HEAD)
    q_scale = HEAD ** (-0.5)
    flat_qkv = joined_qkv(qkv_weight)
    normed_rows = layer_norm(residual, ln_gains[0], ln_shift[0]).astype(jnp.bfloat16)
    normed = lax.all_gather(normed_rows, ("heads", "tensor"), axis=0, tiled=True)
    projected = jnp.dot(normed, flat_qkv, preferred_element_type=jnp.float32)
    queries = (projected[:, :head_cols] * q_scale).astype(jnp.bfloat16).reshape(head_shape)
    key_rows = projected[:, head_cols : 2 * head_cols].astype(jnp.bfloat16).reshape(head_shape)
    value_rows = projected[:, 2 * head_cols :].astype(jnp.bfloat16).reshape(head_shape)
    scores = jnp.einsum("bqhd,bkhd->bhqk", queries, key_rows, preferred_element_type=jnp.float32)
    log_total = jax.nn.logsumexp(scores, axis=-1)
    attn_probs = jax.nn.softmax(scores, axis=-1).astype(jnp.bfloat16)
    mixed_rows = jnp.einsum(
        "bhqk,bkhd->bqhd", attn_probs, value_rows, preferred_element_type=jnp.float32
    )
    mixed_rows = mixed_rows.reshape(group_rows, head_cols).astype(jnp.bfloat16)
    middle = residual + lax.psum_scatter(
        jnp.dot(mixed_rows, out_weight, preferred_element_type=jnp.float32),
        ("heads", "tensor"),
        scatter_dimension=0,
        tiled=True,
    )
    head_full = ()
    normed_two_rows = layer_norm(middle, ln_gains[1], ln_shift[1]).astype(jnp.bfloat16)
    normed_two = lax.all_gather(normed_two_rows, ("heads", "tensor"), axis=0, tiled=True)
    router = jax.nn.softmax(
        jnp.dot(normed_two, router_weight, preferred_element_type=jnp.float32), axis=-1
    )
    gate_values = jnp.take_along_axis(router, named_expert, axis=1) * (slot_rows >= 0)
    places, picked = slot_tables(named_expert, slot_rows, first_expert, local_experts)
    routed = with_zero_row(normed_two)[picked // 2].reshape(local_experts, CAP, widths)
    hidden = jnp.einsum("ecd,edf->ecf", routed, in_weight, preferred_element_type=jnp.float32)
    active = gelu_exact(hidden).astype(jnp.bfloat16)
    result = jnp.einsum("ecf,efd->ecd", active, back_weight, preferred_element_type=jnp.float32)
    flat_result = with_zero_row(result.reshape(local_experts * CAP, widths))
    block_out = middle + lax.psum_scatter(
        (
            flat_result[places[:, 0]] * gate_values[:, 0:1]
            + flat_result[places[:, 1]] * gate_values[:, 1:2]
        ).astype(jnp.bfloat16),
        ("heads", "tensor"),
        scatter_dimension=0,
        tiled=True,
    ).astype(jnp.float32)
    stored = (
        residual,
        middle,
        normed,
        queries,
        key_rows,
        value_rows,
        log_total,
        mixed_rows,
        normed_two_rows,
        router,
        gate_values,
        places,
        picked,
        routed,
        hidden,
        active,
        flat_result,
    )
    return (block_out, stored, head_full)


def backward_block(
    grad_rows, stored, weights, ln_gains, ln_shift, router_weight, named_expert, row_start
):
    qkv_weight, out_weight, in_weight, back_weight = weights
    (
        residual,
        middle,
        normed,
        queries,
        key_rows,
        value_rows,
        log_total,
        mixed_rows,
        normed_two_rows,
        router,
        gate_values,
        places,
        picked,
        routed,
        hidden,
        active,
        flat_result,
    ) = stored
    own_rows, widths = residual.shape
    group_rows = named_expert.shape[0]
    head_cols = qkv_weight.shape[2]
    local_experts = in_weight.shape[0]
    expert_count = router.shape[1]
    q_scale = HEAD ** (-0.5)
    flat_qkv = joined_qkv(qkv_weight)
    grad_moe = lax.all_gather(
        grad_rows.astype(jnp.bfloat16), ("heads", "tensor"), axis=0, tiled=True
    )
    back_rows = with_zero_row(grad_moe)[picked // 2].astype(jnp.float32)
    gate_slots = with_zero_row(gate_values.reshape(-1))[picked]
    gate_grad_slots = jnp.sum(back_rows * flat_result[:-1], axis=1)
    gate_grads = with_zero_row(gate_grad_slots)[places]
    expert_range = jnp.arange(expert_count, dtype=jnp.int32)
    router_part = jnp.sum(
        gate_grads[:, :, None]
        * (named_expert[:, :, None] == expert_range[None, None, :]).astype(jnp.float32),
        axis=1,
    )
    grad_result = (
        (gate_slots[:, None] * back_rows).astype(jnp.bfloat16).reshape(local_experts, CAP, widths)
    )
    grad_active = jnp.einsum(
        "ecd,efd->ecf", grad_result, back_weight, preferred_element_type=jnp.float32
    )
    gelu_value, gelu_pull = jax.vjp(gelu_exact, hidden)
    grad_hidden = gelu_pull(grad_active)[0].astype(jnp.bfloat16)
    back_grad = jnp.einsum("ecf,ecd->efd", active, grad_result, preferred_element_type=jnp.float32)
    in_grad = jnp.einsum("ecd,ecf->edf", routed, grad_hidden, preferred_element_type=jnp.float32)
    grad_routed = jnp.einsum(
        "ecf,edf->ecd", grad_hidden, in_weight, preferred_element_type=jnp.float32
    )
    grad_routed = with_zero_row(grad_routed.reshape(local_experts * CAP, widths))
    token_part = grad_routed[places[:, 0]] + grad_routed[places[:, 1]]
    grad_normed_two, router_rows = (
        lax.psum_scatter(token_part, ("heads", "tensor"), scatter_dimension=0, tiled=True),
        lax.psum_scatter(router_part, ("heads", "tensor"), scatter_dimension=0, tiled=True),
    )
    router_own = lax.dynamic_slice_in_dim(router, row_start, own_rows, 0)
    grad_logits = (
        router_own * (router_rows - jnp.sum(router_own * router_rows, axis=-1, keepdims=True))
    ).astype(jnp.bfloat16)
    router_grad = jnp.einsum(
        "td,te->de", normed_two_rows, grad_logits, preferred_element_type=jnp.float32
    )
    grad_normed_two = grad_normed_two + jnp.einsum(
        "te,de->td", grad_logits, router_weight, preferred_element_type=jnp.float32
    )
    norm_value, norm_pull = jax.vjp(layer_norm, middle, ln_gains[1], ln_shift[1])
    grad_middle, gain_two, shift_two = norm_pull(grad_normed_two)
    grad_middle = grad_middle + grad_rows
    grad_attn = lax.all_gather(
        grad_middle.astype(jnp.bfloat16), ("heads", "tensor"), axis=0, tiled=True
    )
    out_grad = jnp.einsum("tc,td->cd", mixed_rows, grad_attn, preferred_element_type=jnp.float32)
    grad_mixed = jnp.einsum("td,cd->tc", grad_attn, out_weight, preferred_element_type=jnp.float32)
    grad_mixed = grad_mixed.astype(jnp.bfloat16).reshape(queries.shape)
    scores = jnp.einsum("bqhd,bkhd->bhqk", queries, key_rows, preferred_element_type=jnp.float32)
    attn_probs = jnp.exp(scores - log_total[..., None])
    grad_values = jnp.einsum(
        "bhqk,bqhd->bkhd",
        attn_probs.astype(jnp.bfloat16),
        grad_mixed,
        preferred_element_type=jnp.float32,
    )
    grad_probs = jnp.einsum(
        "bqhd,bkhd->bhqk", grad_mixed, value_rows, preferred_element_type=jnp.float32
    )
    grad_scores = (
        attn_probs * (grad_probs - jnp.sum(attn_probs * grad_probs, axis=-1, keepdims=True))
    ).astype(jnp.bfloat16)
    grad_queries = jnp.einsum(
        "bhqk,bkhd->bqhd", grad_scores, key_rows, preferred_element_type=jnp.float32
    )
    grad_keys = jnp.einsum(
        "bhqk,bqhd->bkhd", grad_scores, queries, preferred_element_type=jnp.float32
    )
    grad_projected = jnp.concatenate(
        [
            grad_queries.reshape(group_rows, head_cols),
            grad_keys.reshape(group_rows, head_cols),
            grad_values.reshape(group_rows, head_cols),
        ],
        axis=1,
    ).astype(jnp.bfloat16)
    qkv_flat_grad = jnp.einsum(
        "td,tc->dc", normed, grad_projected, preferred_element_type=jnp.float32
    )
    column_scale = jnp.concatenate(
        [jnp.full((head_cols,), q_scale, jnp.float32), jnp.ones((2 * head_cols,), jnp.float32)]
    )
    qkv_grad = jnp.transpose(
        (qkv_flat_grad * column_scale).reshape(widths, 3, head_cols), (1, 0, 2)
    )
    query_term = (
        jnp.einsum(
            "tc,dc->td",
            grad_projected[:, :head_cols],
            flat_qkv[:, :head_cols],
            preferred_element_type=jnp.float32,
        )
        * q_scale
    )
    grad_normed = lax.psum_scatter(
        query_term
        + jnp.einsum(
            "tc,dc->td",
            grad_projected[:, head_cols:],
            flat_qkv[:, head_cols:],
            preferred_element_type=jnp.float32,
        ),
        ("heads", "tensor"),
        scatter_dimension=0,
        tiled=True,
    )
    first_value, first_pull = jax.vjp(layer_norm, residual, ln_gains[0], ln_shift[0])
    grad_input, gain_one, shift_one = first_pull(grad_normed)
    grad_input = grad_input + grad_middle
    matrix_grads = (qkv_grad, out_grad, in_grad, back_grad)
    small_grads = (jnp.stack([gain_one, gain_two]), jnp.stack([shift_one, shift_two]), router_grad)
    return (grad_input, matrix_grads, small_grads)


def on_device(
    tokens,
    cotangent,
    image_counts,
    w_qkv,
    w_out,
    ln_gain,
    ln_bias,
    w_router,
    w_in,
    w_back,
    expert_ids,
    slots,
):
    own_rows = tokens.shape[0]
    row_start = lax.axis_index(("heads", "tensor")) * own_rows
    first_expert = lax.axis_index("heads") * w_in.shape[1]
    residual = tokens.astype(jnp.float32)
    head_list = []
    block_index = 0
    weights = (
        lax.all_gather(w_qkv[block_index], "fsdp", axis=1, tiled=True),
        lax.all_gather(w_out[block_index], "fsdp", axis=1, tiled=True),
        lax.all_gather(w_in[block_index], "fsdp", axis=1, tiled=True),
        lax.all_gather(w_back[block_index], "fsdp", axis=2, tiled=True),
    )
    residual, stored, head_full = forward_block(
        residual,
        weights,
        ln_gain[block_index],
        ln_bias[block_index],
        w_router[block_index],
        expert_ids[block_index],
        slots[block_index],
        first_expert,
    )
    stored_list = [stored]
    head_list.append(head_full)
    image_index = (row_start + jnp.arange(own_rows, dtype=jnp.int32)) // SEQ
    live_rows = (image_index < image_counts[0]).astype(jnp.float32)
    grad_rows = cotangent.astype(jnp.float32) * live_rows[:, None]
    matrix_list = [None] * LAYERS
    small_list = [None] * LAYERS
    for block_index in reversed(range(LAYERS)):
        weights = (
            lax.all_gather(w_qkv[block_index], "fsdp", axis=1, tiled=True),
            lax.all_gather(w_out[block_index], "fsdp", axis=1, tiled=True),
            lax.all_gather(w_in[block_index], "fsdp", axis=1, tiled=True),
            lax.all_gather(w_back[block_index], "fsdp", axis=2, tiled=True),
        )
        grad_rows, matrix_grads, small_grads = backward_block(
            grad_rows,
            stored_list[block_index],
            weights,
            ln_gain[block_index],
            ln_bias[block_index],
            w_router[block_index],
            expert_ids[block_index],
            row_start,
        )
        matrix_list[block_index] = (
            lax.psum_scatter(matrix_grads[0], "fsdp", scatter_dimension=1, tiled=True),
            lax.psum_scatter(matrix_grads[1], "fsdp", scatter_dimension=1, tiled=True),
            lax.psum_scatter(matrix_grads[2], "fsdp", scatter_dimension=1, tiled=True),
            lax.psum_scatter(matrix_grads[3], "fsdp", scatter_dimension=2, tiled=True),
        )
        small_list[block_index] = small_grads
    gain_grads, shift_grads, router_grads = lax.psum(
        (
            jnp.stack([entry[0] for entry in small_list]),
            jnp.stack([entry[1] for entry in small_list]),
            jnp.stack([entry[2] for entry in small_list]),
        ),
        ("fsdp", "heads", "tensor"),
    )
    qkv_grads = jnp.stack([entry[0] for entry in matrix_list])
    out_grads = jnp.stack([entry[1] for entry in matrix_list])
    in_grads = jnp.stack([entry[2] for entry in matrix_list])
    back_grads = jnp.stack([entry[3] for entry in matrix_list])
    return (
        residual.astype(jnp.bfloat16),
        grad_rows,
        qkv_grads,
        out_grads,
        gain_grads,
        shift_grads,
        router_grads,
        in_grads,
        back_grads,
    )


ROWS = -(-SEQ // 16) * 16
MESH = pl.DeviceIdType.MESH
F32, BF16 = jnp.float32, jnp.bfloat16
NN, NT, TN = (((1,), (0,)), ((), ())), (((1,), (1,)), ((), ())), (((0,), (0,)), ((), ()))


def mm(left, right, dims=NN):
    return lax.dot_general(left, right, dims, preferred_element_type=F32)


def whole(index, size):
    return pl.ds(pl.multiple_of(index * size, size), size)


def normal_parts(value):
    centred = value - jnp.mean(value, axis=-1, keepdims=True)
    scale = lax.rsqrt(jnp.mean(centred * centred, axis=-1, keepdims=True) + 1e-06)
    return centred * scale, scale


def normal_pull(grad, unit, scale, gains):
    grad_unit = grad * gains
    mean_grad = jnp.mean(grad_unit, axis=-1, keepdims=True)
    mean_both = jnp.mean(grad_unit * unit, axis=-1, keepdims=True)
    return scale * (grad_unit - mean_grad - unit * mean_both)


def gelu_parts(value):
    size = jnp.abs(value)
    step = 1.0 / (1.0 + 0.3275911 * 2.0**-0.5 * size)
    bell = jnp.exp(-0.5 * (value * value))
    series = 1.061405429 * step - 1.453152027
    series = series * step + 1.421413741
    series = series * step - 0.284496736
    series = series * step + 0.254829592
    tail = 0.5 * series * step * bell
    share = jnp.where(value < 0, tail, 1.0 - tail)
    return value * share, share + value * (bell * 0.3989422804014327)


class Exchange:
    def __init__(self, source, target, device, landing, send, recv):
        self.out = pltpu.make_async_remote_copy(
            source, target, send, recv, device_id=device, device_id_type=MESH
        )
        self.into = pltpu.make_async_remote_copy(
            landing, landing, send, recv, device_id=device, device_id_type=MESH
        )

        self.open = [True, True]
        self.out.start()

    def arrived(self):
        if self.open[0]:
            self.into.wait_recv()
        self.open[0] = False

    def sent(self):
        if self.open[1]:
            self.out.wait_send()
        self.open[1] = False

    def finish(self):
        self.arrived()
        self.sent()


class Kept:
    def __init__(self, source, target, semaphore):
        self.copy = pltpu.make_async_copy(source, target, semaphore)
        self.open = True
        self.copy.start()

    def arrived(self):
        if self.open:
            self.copy.wait()
        self.open = False

    sent = finish = arrived


def block_kernel(depth_z, images, local_count, refs):
    H = depth_z
    (
        tokens, cot, counts, wq, wo, gain, bias, wr, win_hbm, wback_hbm, named_in, slots_in,
        out, tgrad, wqg, wog, lng, lnb, wrg, gin_out, gback_out,
        stage, prow, wbuf, win, wback, rows_grad, rows_norm, big, wide,
        xsend, gsend, xrows, grows, xback, gback,
        normed, qkv, probs, mixed, middle, grad_mid, logit_grad,
        sib_out, sib_in, z_out, z_in, own_sum,
        att_in, plane_in, line_out, line_in,
        small_c, small_p, small_z, route_out, route_in, route_z, route_all,
        send_sems, recv_sems, local_sems,
    ) = refs
    own = images * ROWS
    width = tokens.shape[1]
    half = width // 128
    f, h, t = (lax.axis_index(name) for name in ("fsdp", "heads", "tensor"))
    s = 1 - t
    fx = [f, f + 1 - 2 * lax.rem(f, 2), lax.rem(f + 2, 4), 3 - f]
    hz = [lax.rem(h + d, H) for d in range(H)]
    hfrom = [lax.rem(h + H - d, H) for d in range(H)]
    after, before, across = lax.rem(2 * h + 1, 5), lax.rem(3 * h + 2, 5), 3 - h
    counter = [0]
    pending = []

    def exchange(source, target, device, landing):
        index = counter[0]
        counter[0] += 1
        made = Exchange(
            source, target, device, landing, send_sems.at[index], recv_sems.at[index]
        )
        pending.append(made)
        return made

    local_counter = [0]

    def kept(source, target):
        made = Kept(source, target, local_sems.at[local_counter[0]])
        local_counter[0] += 1
        pending.append(made)
        return made

    barrier = pltpu.get_barrier_semaphore()
    peers = [(f, hz[d], t) for d in range(1, H)] + [(f, h, s)]
    peers += [(fx[d], h, c) for d in range(1, 4) for c in (t, s)]
    for peer in peers:
        pl.semaphore_signal(barrier, inc=1, device_id=peer, device_id_type=MESH)

    for i in range(3):
        wbuf[i, h, t, :, whole(f, 128)] = wq[i]
    wbuf[3, h, t, :, whole(f, 128)] = wo[...]
    pl.semaphore_wait(barrier, len(peers))

    first = [
        exchange(*[wbuf.at[:, h, t, :, whole(f, 128)]] * 2, (f, hz[d], t),
                 wbuf.at[:, hfrom[d], t, :, whole(f, 128)])
        for d in range(1, H)
    ]

    depth, span = win_hbm.shape[1], win_hbm.shape[2]

    def move_in(d, c):
        landing = win.at[whole(fx[d], depth), whole(c, span)]
        target = win.at[whole(f, depth), whole(t, span)]
        return exchange(win_hbm.at[fx[d] * 2 + c], target, (fx[d], h, c), landing)

    def move_back(d, c):
        landing = wback.at[whole(c, span), whole(fx[d], depth)]
        target = wback.at[whole(t, span), whole(f, depth)]
        return exchange(wback_hbm.at[fx[d] * 2 + c], target, (fx[d], h, c), landing)

    expert_moves = [move_in(d, c) for d, c in ((1, t), (2, t), (1, s), (2, s))]
    mine = [
        kept(win_hbm.at[f * 2 + t], win.at[whole(f, depth), whole(t, span)]),
        kept(wback_hbm.at[f * 2 + t], wback.at[whole(t, span), whole(f, depth)]),
    ]

    row_index = lax.broadcasted_iota(jnp.int32, (ROWS, 1), 0)

    def image(source, b):
        if b == 0:
            stage[0 : images * SEQ, :] = source[...].astype(F32)
        return jnp.where(row_index < SEQ, stage[b * SEQ : b * SEQ + ROWS, :], 0.0)

    for b in range(images):
        live = ((h * 2 + t) * images + b < counts[0]).astype(F32)
        rows_grad[h * 2 + t, b * ROWS : (b + 1) * ROWS, :] = (image(cot, b) * live).astype(BF16)

    parts = [slice(0, own // 2), slice(own // 2, own)]

    def hop(rows, line, part, to, source):
        here = rows.at[line * 2 + t, parts[part]]
        return exchange(here, here, (f, to, t), rows.at[source * 2 + t, parts[part]])

    def beside(rows, line):
        here = rows.at[line * 2 + t, 0:own]
        return exchange(here, here, (f, h, s), rows.at[line * 2 + s, 0:own])

    class Spread:
        def __init__(self, rows):
            self.rows = rows
            self.down = [hop(rows, h, 0, after, before), None]
            self.up = [None, hop(rows, h, 1, before, after)]
            self.near = [beside(rows, h)]

        def second(self):
            self.down[1] = hop(self.rows, h, 1, after, before)
            self.up[0] = hop(self.rows, h, 0, before, after)

        def relay(self):
            self.down[0].arrived()
            self.far = [hop(self.rows, before, 0, after, across)]
            self.up[1].arrived()
            self.far.append(hop(self.rows, after, 1, before, across))

        def share(self):
            self.down[1].arrived()
            self.near.append(beside(self.rows, before))
            self.up[0].arrived()
            self.near.append(beside(self.rows, after))

        def close(self):
            for move in self.far:
                move.arrived()
            self.near.append(beside(self.rows, across))

        def blocks(self):
            lines = [h, before, after, across]
            moves = self.near + [None] * (4 - len(self.near))
            return [(line * 2 + t, None) for line in lines] + [
                (line * 2 + s, move) for line, move in zip(lines, moves)
            ]

        def sent(self):
            for move in self.down + self.up + self.far + self.near:
                move.sent()

    for b in range(images):
        unit, _ = normal_parts(image(tokens, b))
        normed[b * ROWS : (b + 1) * ROWS, :] = (unit * gain[0:1] + bias[0:1]).astype(BF16)

    for step in first:
        step.arrived()
    grad_spread = Spread(rows_grad)
    second = [
        exchange(*[wbuf.at[:, :, t, :, whole(f, 128)]] * 2, (fx[d], h, t),
                 wbuf.at[:, :, t, :, whole(fx[d], 128)])
        for d in range(1, 4)
    ]

    relative = named_in[...] - h * local_count
    wanted = (slots_in[...] >= 0) & (relative >= 0) & (relative < local_count)
    wanted = wanted & (lax.rem(relative + 2 * local_count, 2) == t)
    places = jnp.where(wanted, lax.div(relative, 2) * CAP + slots_in[...], -1)
    reach = -(-(images * ROWS) // 128) * 128 + 128
    tail = jnp.full((2, reach), -1, jnp.int32)
    places = jnp.concatenate([places, tail], axis=1)[:, 0 : places.shape[1] // 128 * 128 + reach]
    place_lane = lax.broadcasted_iota(jnp.int32, (2, reach), 1)
    for b in range(2 * H):
        rows = jnp.full((2, reach), -1, jnp.int32)
        for i in range(images):
            begin = (b * images + i) * SEQ - i * ROWS
            base = max(begin // 128, 0) * 128
            window = pltpu.roll(places[:, base : base + reach], (base - begin) % reach, 1)
            inside = (place_lane >= i * ROWS) & (place_lane < i * ROWS + SEQ)
            rows = jnp.where(inside, window, rows)
        prow[b, 0:2, :] = rows[:, 0 : prow.shape[2]]

    def mark_slots(b):
        for part in range(4):
            spot = lax.broadcasted_iota(jnp.int32, (CAP, own), 0) + CAP * part
            named = (prow[b, 0:1, 0:own] == spot) | (prow[b, 1:2, 0:own] == spot)
            big[b, part * CAP : (part + 1) * CAP, 0:own] = jnp.where(named, 1.0, 0.0).astype(BF16)

    grad_spread.second()
    pl.loop(0, H)(mark_slots)
    grad_spread.relay()
    pl.loop(H, 2 * H)(mark_slots)
    for step in second:
        step.arrived()
    third = exchange(*[wbuf.at[:, :, t]] * 2, (f, h, s), wbuf.at[:, :, s])

    for d, c in ((3, t), (3, s), (0, s)):
        expert_moves.append(move_in(d, c))
    for d, c in ((1, t), (2, t), (1, s), (2, s), (3, t), (3, s), (0, s)):
        expert_moves.append(move_back(d, c))

    grad_spread.share()
    third.arrived()

    for i in range(3):
        part = mm(normed[...], wbuf[i].reshape(width, width), NT)
        if i == 0:
            part = part * HEAD ** (-0.5)
        qkv[:, i * width : (i + 1) * width] = part.astype(BF16)
    lane = lax.broadcasted_iota(jnp.int32, (1, 128), 1)
    sides = [jnp.where(lane < HEAD, 1.0, 0.0).astype(BF16), jnp.where(lane < HEAD, 0.0, 1.0).astype(BF16)]
    key_index = lax.broadcasted_iota(jnp.int32, (1, ROWS), 1)

    def pair_of(index):
        b, pair = index // half, lax.rem(index, half)
        rows = whole(b, ROWS)
        cols = [whole(pair + i * half, 128) for i in range(3)]
        return rows, cols

    @pl.loop(0, images * half)
    def _(index):
        rows, cols = pair_of(index)
        query, key, value = (qkv[rows, col] for col in cols)
        total = jnp.zeros((ROWS, 128), F32)
        for side in range(2):
            score = mm(query * sides[side], key, NT)
            score = jnp.where(key_index < SEQ, score, -1e30)
            score = jnp.exp(score - jnp.max(score, axis=-1, keepdims=True))
            prob = score / jnp.sum(score, axis=-1, keepdims=True)
            probs[index * 2 + side] = prob
            total += mm(prob.astype(BF16), value * sides[side])
        mixed[rows, cols[0]] = total.astype(BF16)

    for b in range(images):
        rows = slice(b * ROWS, (b + 1) * ROWS)
        value = image(tokens, b) + mm(mixed[rows, :], wbuf[3].reshape(width, width))
        middle[rows, :] = value
        unit, _ = normal_parts(value)
        rows_norm[h * 2 + t, rows, :] = (unit * gain[1:2] + bias[1:2]).astype(BF16)

    norm_spread = Spread(rows_norm)
    grad_spread.close()

    def accumulate(rows, b, begin):
        for part in range(4):
            span_rows = slice(part * CAP, (part + 1) * CAP)
            value = mm(big[b, span_rows, 0:own], rows[b, 0:own])
            wide[span_rows, :] = value if begin else wide[span_rows, :] + value

    def accumulate_all(spread, order):
        blocks = spread.blocks()
        for place in order:
            b, move = blocks[place]
            if move is not None:
                move.arrived()
            accumulate(spread.rows, b, place == 0)

    def pack(send):
        for part in range(4):
            send[part] = wide[part * CAP : (part + 1) * CAP, :].astype(BF16)

    def to_group(d, send, landing):
        return exchange(send.at[fx[d]], landing.at[f], (fx[d], h, t), landing.at[fx[d]])

    def dispatch(send, landing, last=4):
        landing[f] = send[f]
        return [None] + [to_group(d, send, landing) for d in range(1, last)]

    accumulate_all(grad_spread, (0, 1, 2, 3))
    norm_spread.second()
    accumulate_all(grad_spread, (4, 5, 6, 7))
    pack(gsend)
    norm_spread.relay()
    grad_moved = dispatch(gsend, grows)
    norm_spread.share()
    accumulate_all(norm_spread, (0, 1, 2, 4, 5, 6))
    norm_spread.close()
    accumulate_all(norm_spread, (3, 7))
    pack(xsend)
    norm_moved = dispatch(xsend, xrows, 3)

    expert = h * local_count + f * 2 + t
    router_lane = lax.broadcasted_iota(jnp.int32, (1, wr.shape[0]), 1)
    chosen = (router_lane == expert).astype(F32)
    chunk = 512
    chunks = win.shape[1] // chunk
    for move in mine + expert_moves:
        move.arrived()
    back_moves = []
    for d in range(4):
        group = fx[d]
        here = whole(group, CAP)
        if d:
            norm_moved[d].arrived()
        rows = xrows[group]
        result = jnp.zeros((CAP, width), F32)
        for c in range(chunks):
            value, slope = gelu_parts(mm(rows, win[:, c * chunk : (c + 1) * chunk]))
            value = value.astype(BF16)
            big[c, here, :] = value
            wide[c * CAP : (c + 1) * CAP, :] = slope
            result += mm(value, wback[c * chunk : (c + 1) * chunk, :])
        logits = mm(rows, wr[...], NT)
        odds = jnp.exp(logits - jnp.max(logits, axis=-1, keepdims=True))
        odds = odds / jnp.sum(odds, axis=-1, keepdims=True)
        gate = jnp.sum(odds * chosen, axis=-1, keepdims=True)
        if d:
            grad_moved[d].finish()
            norm_moved[d].sent()
        gsend[group] = (gate * result).astype(BF16)
        row_grad = grows[group].astype(F32)
        gate_grad = jnp.sum(row_grad * result, axis=-1, keepdims=True)
        result_grad = (gate * row_grad).astype(BF16)
        grows[group] = result_grad
        logit = (gate_grad * gate * (chosen - odds)).astype(BF16)
        logit_grad[here, :] = logit
        parts_grad = []
        for c in range(chunks):
            grad = mm(result_grad, wback[c * chunk : (c + 1) * chunk, :], NT)
            grad = (grad * wide[c * CAP : (c + 1) * CAP, :]).astype(BF16)
            big[4 + c, here, :] = grad
            parts_grad.append(grad)
        total = mm(logit, wr[...]) + mm(jnp.concatenate(parts_grad, axis=1), win[...], NT)
        if d:
            xsend[group] = total.astype(BF16)
            back_moves.append(to_group(d, xsend, xback))
        else:
            xback[f] = total.astype(BF16)
            norm_moved.append(to_group(3, xsend, xrows))

    grad_spread.sent()
    norm_spread.sent()
    flat_rows = xrows[...].reshape(4 * CAP, width)
    flat_grad = grows[...].reshape(4 * CAP, width)
    for c in range(chunks):
        rows_grad[c] = mm(flat_rows, big[4 + c], TN).astype(BF16)
        rows_norm[c] = mm(big[c], flat_grad, TN).astype(BF16)
    route = mm(logit_grad[...], flat_rows, TN)
    share_rows = wr.shape[0] // 8
    for j in range(8):
        route_out[j, 0:share_rows, :] = route[j * share_rows : (j + 1) * share_rows]

    for move in back_moves:
        move.arrived()
    out_moves = dispatch(gsend, gback)[1:]

    halves = chunks // 2

    def to_owner(d, c, part, back):
        device, one = (fx[d], h, c), d == 0 and c is t
        span_part = slice(part * chunk, (part + 1) * chunk)
        if back:
            source = rows_norm.at[c * halves + part, :, whole(fx[d], depth)]
            target = gback_out.at[f * 2 + t, span_part]
            landing = gback_out.at[fx[d] * 2 + c, span_part]
        else:
            source = rows_grad.at[c * halves + part, whole(fx[d], depth), :]
            target = gin_out.at[f * 2 + t, :, span_part]
            landing = gin_out.at[fx[d] * 2 + c, :, span_part]
        if one:
            kept(source, target)
        else:
            exchange(source, target, device, landing)

    def to_owners(part, back):
        for d in (1, 2, 3, 0):
            for c in (t, s):
                to_owner(d, c, part, back)

    plane_peers = [(d, c) for d in range(4) for c in ((t, s) if d else (s,))]
    route_in[f * 2 + t] = route_out[f * 2 + t]
    route_moves = [
        exchange(route_out.at[fx[d] * 2 + c], route_in.at[f * 2 + t], (fx[d], h, c), route_in.at[fx[d] * 2 + c])
        for d, c in plane_peers
    ]

    def share(b, back):
        spots = jnp.transpose(prow[b])[0:own]
        slot = lax.broadcasted_iota(jnp.int32, (own, 4 * CAP), 1)
        named = (spots[:, 0:1] == slot) | (spots[:, 1:2] == slot)
        return mm(jnp.where(named, 1.0, 0.0).astype(BF16), back[...].reshape(4 * CAP, width))

    class Gather:
        def __init__(self, which, back, near_out, far_out):
            self.which, self.back = which, back
            self.near_out, self.far_out = near_out, far_out
            self.lines = [across, after, before, h]
            self.near = []

        def give(self, place):
            line = self.lines[place]
            self.near_out(place)[...] = share(line * 2 + s, self.back).astype(BF16)
            landing = sib_in.at[self.which, place]
            self.near.append(exchange(self.near_out(place), landing, (f, h, s), landing))

        def take(self, place):
            value = share(self.lines[place] * 2 + t, self.back)
            self.near[place].arrived()
            value = value + sib_in[self.which, place].astype(F32)
            if place == 3:
                own_sum[self.which] = value
            else:
                self.far_out(place)[...] = value.astype(BF16)

        def hop(self, place, part, to, slot):
            landing = z_in.at[self.which, slot, parts[part]]
            return exchange(self.far_out(place).at[parts[part]], landing, (f, to, t), landing)

        def start(self):
            self.first = [self.hop(0, 0, after, 0), self.hop(0, 1, before, 0)]

        def direct(self, place):
            part, to = ((1, after), (0, before))[place - 1]
            self.last = getattr(self, "last", []) + [self.hop(place, part, to, place)]

        def relay(self):
            for place, part, to in ((1, 0, after), (2, 1, before)):
                self.first[part].arrived()
                rows = self.far_out(place).at[parts[part]]
                passed = z_in[self.which, 0, parts[part], :].astype(F32)
                rows[...] = (rows[...].astype(F32) + passed).astype(BF16)
                self.last.append(self.hop(place, part, to, place))

        def total(self, rows):
            for move in self.last:
                move.arrived()
            total = own_sum[self.which, rows, :]
            for slot in (1, 2):
                total = total + z_in[self.which, slot, rows, :].astype(F32)
            return total

    def to_owners_first():
        to_owners(0, True)
        to_owners(1, True)
        to_owners(0, False)

    norm_sums = Gather(0, xback, lambda place: sib_out.at[place], lambda place: z_out.at[place])
    norm_sums.give(0)
    norm_sums.take(0)
    norm_sums.start()
    norm_sums.give(1)
    norm_sums.give(2)
    norm_sums.take(1)
    norm_sums.direct(1)
    norm_sums.take(2)
    norm_sums.direct(2)
    norm_sums.give(3)
    norm_sums.take(3)
    for move in out_moves:
        move.arrived()
    to_owners_first()
    out_sums = Gather(
        1, gback, lambda place: big.at[place, 0:own], lambda place: big.at[4 + place, 0:own]
    )
    out_sums.give(0)
    out_sums.take(0)
    for place in range(1, 4):
        out_sums.give(place)
    norm_sums.relay()
    for place in range(1, 4):
        out_sums.take(place)

    for move in route_moves:
        move.arrived()
    route = route_in[0, 0:share_rows, :]
    for j in range(1, 8):
        route = route + route_in[j, 0:share_rows, :]
    route_z[h, 0:share_rows, :] = route
    route_line = [
        exchange(route_z.at[h], route_z.at[h], (f, hz[d], t), route_z.at[hfrom[d]]) for d in range(1, H)
    ]

    for move in norm_sums.last:
        move.arrived()
    out_sums.start()
    small_c[t] = jnp.zeros(small_c.shape[1:], F32)
    for b in range(images):
        rows = slice(b * ROWS, (b + 1) * ROWS)
        grad = norm_sums.total(rows)
        unit, scale = normal_parts(middle[rows, :])
        small_c[t, 1:2] += jnp.sum(grad * unit, axis=0, keepdims=True)
        small_c[t, 3:4] += jnp.sum(grad, axis=0, keepdims=True)
        live = ((h * 2 + t) * images + b < counts[0]).astype(F32)
        grad = normal_pull(grad, unit, scale, gain[1:2]) + image(cot, b) * live
        grad_mid[rows, :] = grad

    out_sums.direct(1)
    out_sums.direct(2)

    for move in back_moves:
        move.sent()
    low = grad_mid[...].astype(BF16)
    count = H * 2 * 64
    wide[3 * count : 4 * count, :] = mm(mixed[...], low, TN)

    def wide_rows(i, other, core):
        return whole((i * H + other) * 2 + core, 64)

    def core_sums(span_i, others):
        for i in span_i:
            for other in others:
                xsend[i, whole(other, 64), :] = wide[wide_rows(i, other, s), :].astype(BF16)
        here = (slice(span_i.start, span_i.stop), whole(others[0], 64))
        if len(others) > 1:
            here = (here[0], slice(0, H * 64))
        landing = att_in.at[here]
        return here, exchange(xsend.at[here], landing, (f, h, s), landing)

    def plane_sums(span_i, others, near):
        here, move = near
        move.finish()
        for i in span_i:
            for other in others:
                place, low_rows = wide_rows(i, other, t), whole(other, 64)
                value = wide[place, :] + att_in[i, low_rows, :].astype(F32)
                wide[place, :] = value
                xsend[i, low_rows, :] = value.astype(BF16)
        return [
            exchange(
                xsend.at[(*here, whole(fx[d], 128))], plane_in.at[(f, *here)],
                (fx[d], h, t), plane_in.at[(fx[d], *here)],
            )
            for d in range(1, 4)
        ]

    def own_columns(i, other):
        value = wide[wide_rows(i, other, t), whole(f, 128)]
        for d in range(1, 4):
            value = value + plane_in[fx[d], i, whole(other, 64), :].astype(F32)
        return value

    last_near = core_sums(range(3, 4), list(range(H)))
    mixed[...] = mm(low, wbuf[3].reshape(width, width), NT).astype(BF16)

    def attention_back(index):
        rows, cols = pair_of(index)
        query, key, value = (qkv[rows, col] for col in cols)
        pulled = mixed[rows, cols[0]]
        grads = [jnp.zeros((ROWS, 128), F32) for _ in range(3)]
        for side in range(2):
            prob = probs[index * 2 + side]
            one = pulled * sides[side]
            prob_grad = mm(one, value, NT)
            grads[2] += mm(prob.astype(BF16), one, TN)
            inner = jnp.sum(prob * prob_grad, axis=-1, keepdims=True)
            score_grad = (prob * (prob_grad - inner)).astype(BF16)
            grads[0] += mm(score_grad, key * sides[side])
            grads[1] += mm(score_grad, query * sides[side], TN)
        grads[0] = grads[0] * HEAD ** (-0.5)
        for grad, col in zip(grads, cols):
            qkv[rows, col] = grad.astype(BF16)

    order = [hz[1], hz[2], hz[3], hz[0]]
    nears, planes = [], []
    for turn, other in enumerate(order):
        pl.loop(0, images)(lambda b, other=other: attention_back(b * half + other))
        for i in range(3):
            rows = pl.ds(pl.multiple_of((i * H + other) * 128, 128), 128)
            wide[rows, :] = mm(qkv[:, whole(i * half + other, 128)], normed[...], TN)
        nears.append(core_sums(range(3), [other]))
        if turn == 0:
            last_plane = plane_sums(range(3, 4), list(range(H)), last_near)
        else:
            planes.append(plane_sums(range(3), [order[turn - 1]], nears[turn - 1]))
    out_sums.relay()

    for b in range(images):
        rows = slice(b * ROWS, (b + 1) * ROWS)
        grad = jnp.zeros((ROWS, width), F32)
        for i in range(3):
            grad += mm(qkv[rows, i * width : (i + 1) * width], wbuf[i].reshape(width, width))
        unit, scale = normal_parts(image(tokens, b))
        small_c[t, 0:1] += jnp.sum(grad * unit, axis=0, keepdims=True)
        small_c[t, 2:3] += jnp.sum(grad, axis=0, keepdims=True)
        grad = normal_pull(grad, unit, scale, gain[0:1]) + grad_mid[rows, :]
        tgrad[b * SEQ : (b + 1) * SEQ, :] = grad[0:SEQ]
    small_near = exchange(small_c.at[t], small_c.at[t], (f, h, s), small_c.at[s])

    planes.append(plane_sums(range(3), [order[3]], nears[3]))
    small_near.arrived()
    small_p[f] = small_c[0] + small_c[1]
    small_plane = [
        exchange(small_p.at[f], small_p.at[f], (fx[d], h, t), small_p.at[fx[d]]) for d in range(1, 4)
    ]
    for move in route_line:
        move.arrived()
    route = route_z[0]
    for d in range(1, H):
        route = route + route_z[d]
    route_all[f * 2 + t] = route
    route_last = [
        exchange(route_all.at[f * 2 + t], route_all.at[f * 2 + t], (fx[d], h, c), route_all.at[fx[d] * 2 + c])
        for d, c in plane_peers
    ]

    for move in last_plane:
        move.arrived()
    line = []
    for turn in range(3):
        for move in planes[turn]:
            move.arrived()
        other = order[turn]
        for i in range(4):
            line_out[other, i] = own_columns(i, other).astype(BF16)
        d = turn + 1
        line.append(
            exchange(line_out.at[other], line_in.at[h], (f, other, t), line_in.at[hfrom[d]])
        )
    for move in planes[3]:
        move.arrived()
    to_owners(1, False)
    for move in small_plane:
        move.arrived()
    small_z[h] = (small_p[0] + small_p[1]) + (small_p[2] + small_p[3])
    small_line = [
        exchange(small_z.at[h], small_z.at[h], (f, hz[d], t), small_z.at[hfrom[d]]) for d in range(1, H)
    ]
    for move in route_last:
        move.arrived()
    for j in range(8):
        wrg[j * share_rows : (j + 1) * share_rows, :] = route_all[j, 0:share_rows, :]

    for b in range(images):
        rows = slice(b * ROWS, (b + 1) * ROWS)
        value = middle[rows, :] + out_sums.total(rows)
        stage[b * SEQ : (b + 1) * SEQ, :] = value[0:SEQ]
    out[...] = stage[0 : images * SEQ, :].astype(BF16)

    for move in line:
        move.arrived()
    for i in range(4):
        value = own_columns(i, h)
        for d in range(1, H):
            value = value + line_in[hfrom[d], i].astype(F32)
        if i < 3:
            wqg[i] = value
        else:
            wog[...] = value
    for move in small_line:
        move.arrived()
    total = small_z[0]
    for d in range(1, H):
        total = total + small_z[d]
    lng[...] = total[0:2]
    lnb[...] = total[2:4]

    for move in pending:
        move.finish()


def finish_kernel(*refs):
    sources, targets = refs[:9], refs[9:18]
    held, wider = refs[18:27], refs[27:29]
    in_sems, out_sems = refs[29], refs[30]
    experts = sources[7].shape[0]
    inward, outward = [], []

    def begin(source, target, semaphores, index):
        copy = pltpu.make_async_copy(source, target, semaphores.at[index])
        copy.start()
        return copy

    for e in range(experts):
        for k in (7, 8):
            index = 7 + 2 * e + k - 7
            inward.append((e, k, index, begin(sources[k].at[e], held[k].at[e], in_sems, index)))
    small = [begin(sources[k], held[k], in_sems, k) for k in range(7)]
    for e, k, index, copy in inward:
        copy.wait()
        wider[k - 7][e] = held[k][e].astype(F32)
        outward.append(begin(wider[k - 7].at[e], targets[k].at[e], out_sems, index))
    for k, copy in enumerate(small):
        copy.wait()
        outward.append(begin(held[k], targets[k], out_sems, k))
    for copy in outward:
        copy.wait()


def fast_device(
    tokens,
    cotangent,
    image_counts,
    w_qkv,
    w_out,
    ln_gain,
    ln_bias,
    w_router,
    w_in,
    w_back,
    expert_ids,
    slots,
):
    H = lax.axis_size("heads")
    own_rows, width = tokens.shape
    images = own_rows // SEQ
    own = images * ROWS
    local_count, depth, span = w_in.shape[1:]
    experts = w_router.shape[2]
    hidden = span * 2
    vmem = pl.BlockSpec(memory_space=pltpu.VMEM)
    smem = pl.BlockSpec(memory_space=pltpu.SMEM)
    anywhere = pl.BlockSpec(memory_space=pl.ANY)
    shape = jax.ShapeDtypeStruct

    def low(*dims):
        return pltpu.VMEM(dims, BF16)

    def full(*dims):
        return pltpu.VMEM(dims, F32)

    outs = pl.pallas_call(
        lambda *refs: block_kernel(H, images, local_count, refs),
        out_shape=(
            shape((own_rows, width), BF16),
            shape((own_rows, width), F32),
            shape((3, 64, depth), F32),
            shape((64, depth), F32),
            shape((2, width), F32),
            shape((2, width), F32),
            shape((experts, width), F32),
            shape((local_count, depth, span), BF16),
            shape((local_count, span, depth), BF16),
        ),
        in_specs=[vmem, vmem, smem, vmem, vmem, vmem, vmem, vmem, anywhere, anywhere, vmem, vmem],
        out_specs=[vmem] * 7 + [anywhere] * 2,
        scratch_shapes=[
            full(images * SEQ + 16, width),
            pltpu.VMEM((2 * H, 8, -(-own // 128) * 128), jnp.int32),
            low(4, H, 2, 64, width),
            low(width, hidden),
            low(hidden, width),
            low(2 * H, 512, width),
            low(2 * H, 512, width),
            low(8, 4 * CAP, 512),
            full(8 * CAP, width),
            low(4, CAP, width),
            low(4, CAP, width),
            low(4, CAP, width),
            low(4, CAP, width),
            low(4, CAP, width),
            low(4, CAP, width),
            low(own, width),
            low(own, 3 * width),
            full(images * width // HEAD, ROWS, ROWS),
            low(own, width),
            full(own, width),
            full(own, width),
            low(4 * CAP, experts),
            low(H, own, width),
            low(2, H, own, width),
            low(3, own, width),
            low(2, 3, own, width),
            full(2, own, width),
            low(4, H * 64, width),
            low(4, 4, H * 64, 128),
            low(H, 4, 64, 128),
            low(H, 4, 64, 128),
            full(2, 8, width),
            full(4, 8, width),
            full(H, 8, width),
            full(8, 8, width),
            full(8, 8, width),
            full(H, 8, width),
            full(8, 8, width),
            pltpu.SemaphoreType.DMA((192,)),
            pltpu.SemaphoreType.DMA((192,)),
            pltpu.SemaphoreType.DMA((16,)),
        ],
        compiler_params=pltpu.CompilerParams(
            collective_id=0, has_side_effects=True, vmem_limit_bytes=62 * 2**20
        ),
        name="block",
    )(
        tokens, cotangent, image_counts, jnp.transpose(w_qkv[0], (0, 2, 1)), w_out[0], ln_gain[0], ln_bias[0],
        jnp.transpose(w_router[0]),
        w_in[0], w_back[0], jnp.transpose(expert_ids[0]), jnp.transpose(slots[0]),
    )
    sems = pltpu.SemaphoreType.DMA((7 + 2 * local_count,))
    outs = pl.pallas_call(
        finish_kernel,
        out_shape=[shape(part.shape, F32 if i >= 7 else part.dtype) for i, part in enumerate(outs)],
        in_specs=[anywhere] * 9,
        out_specs=[anywhere] * 9,
        scratch_shapes=[pltpu.VMEM(part.shape, part.dtype) for part in outs]
        + [full(*part.shape) for part in outs[7:]]
        + [sems, sems],
        compiler_params=pltpu.CompilerParams(vmem_limit_bytes=62 * 2**20),
        name="finish",
    )(*outs)
    block_out, token_grad, qkv_grad, out_grad, gains, shifts, router, in_grad, back_grad = outs
    return (
        block_out,
        token_grad,
        jnp.transpose(qkv_grad, (0, 2, 1))[None],
        out_grad[None],
        gains[None],
        shifts[None],
        jnp.transpose(router)[None],
        in_grad[None],
        back_grad[None],
    )


def solution(mesh):
    def program(*arrays):
        sizes = dict(mesh.shape)
        devices = sizes["fsdp"] * sizes["heads"] * sizes["tensor"]
        own_rows = arrays[0].shape[0] // devices
        one_expert = sizes["fsdp"] == 4 and sizes["tensor"] == 2 and arrays[8].shape[1] == devices
        one_expert = one_expert and sizes["heads"] == 4 and own_rows % (2 * SEQ) == 0
        return placed(mesh, fast_device if one_expert else on_device)(*arrays)

    return program


def placed(mesh, on_device):
    return jax.shard_map(
        on_device,
        mesh=mesh,
        in_specs=(
            P(("fsdp", "heads", "tensor"), None),
            P(("fsdp", "heads", "tensor"), None),
            P("fsdp"),
            P(None, None, "fsdp", ("heads", "tensor")),
            P(None, ("heads", "tensor"), "fsdp"),
            P(),
            P(),
            P(),
            P(None, "heads", "fsdp", "tensor"),
            P(None, "heads", "tensor", "fsdp"),
            P(None, "fsdp", None),
            P(None, "fsdp", None),
        ),
        out_specs=(
            P(("fsdp", "heads", "tensor"), None),
            P(("fsdp", "heads", "tensor"), None),
            P(None, None, "fsdp", ("heads", "tensor")),
            P(None, ("heads", "tensor"), "fsdp"),
            P(),
            P(),
            P(),
            P(None, "heads", "fsdp", "tensor"),
            P(None, "heads", "tensor", "fsdp"),
        ),
        check_vma=False,
    )
```

profile of v0, /device:TPU:0, one launch (start us, length us, event | category | flops | bytes accessed | tf_op | source)
XLA Modules:
  0.0 188.5 jit_solution(15034396717604143338)
XLA Ops:
  1.3 181.3 %block.1 = (bf16[394,512]{1,0:T(8,128)(2,1)}, f32[394,512]{1,0:T(8,128)}, f32[3,64,128]{2,1,0:T(8,128)}, f32[64,128]{1,0:T(8,128)}, f32[2,512]{1,0:T(2,128)}, /*...) custom-call(bf16[394,512]{1,0:T(8,128)(2,1)} %refs_0_.1, ...), custom_call_target="tpu_custom_call" | custom-call | tf_op jit(solution)/shard_map/block/pallas_call | solution.py:1138
  182.6 5.4 %finish.1 = (bf16[394,512]{1,0:T(8,128)(2,1)}, f32[394,512]{1,0:T(8,128)}, f32[3,64,128]{2,1,0:T(8,128)}, f32[64,128]{1,0:T(8,128)}, f32[2,512]{1,0:T(2,128)}, /...) custom-call(bf16[394,512]{1,0:T(8,128)(2,1)} %get-tuple-element.27.refs_0_, ...), custom_call_target="tpu_custom_call" | custom-call | tf_op jit(solution)/shard_map/finish/pallas_call | solution.py:1206
where the time goes:
time: 191 us; the launch traced here: 189 us
  Pallas kernels  187 us (98%)
    pallas_call x1, Pallas kernels, fast_device(): pl.pallas_call(lambda *refs: block_kernel(H, images, local_count, refs),...  181 us
    pallas_call x1, Pallas kernels, fast_device(): pl.pallas_call(finish_kernel, out_shape=[shape(part.shape, F32 if i >= 7...  5.41 us

commit v1 on v0

--- a/solution.py
+++ b/solution.py
@@ -452,8 +452,8 @@
         small_c, small_p, small_z, route_out, route_in, route_z, route_all,
         send_sems, recv_sems, local_sems,
     ) = refs
-    own = images * ROWS
-    width = tokens.shape[1]
+    own_rows, width = tokens.shape
+    flat = -(-own_rows // 16) * 16
     half = width // 128
     f, h, t = (lax.axis_index(name) for name in ("fsdp", "heads", "tensor"))
     s = 1 - t
@@ -523,19 +523,22 @@
             stage[0 : images * SEQ, :] = source[...].astype(F32)
         return jnp.where(row_index < SEQ, stage[b * SEQ : b * SEQ + ROWS, :], 0.0)
 
-    for b in range(images):
-        live = ((h * 2 + t) * images + b < counts[0]).astype(F32)
-        rows_grad[h * 2 + t, b * ROWS : (b + 1) * ROWS, :] = (image(cot, b) * live).astype(BF16)
-
-    parts = [slice(0, own // 2), slice(own // 2, own)]
+    flat_index = lax.broadcasted_iota(jnp.int32, (flat, 1), 0)
+    flat_image = sum((flat_index >= b * SEQ).astype(jnp.int32) for b in range(1, images))
+    living = (flat_index < own_rows) & ((h * 2 + t) * images + flat_image < counts[0])
+    stage[0:own_rows, :] = cot[...].astype(F32)
+    rows_grad[h * 2 + t, 0:flat, :] = jnp.where(living, stage[0:flat, :], 0.0).astype(BF16)
+
+    cut = -(-flat // 32) * 16
+    parts = [slice(0, cut), slice(cut, flat)]
 
     def hop(rows, line, part, to, source):
         here = rows.at[line * 2 + t, parts[part]]
         return exchange(here, here, (f, to, t), rows.at[source * 2 + t, parts[part]])
 
     def beside(rows, line):
-        here = rows.at[line * 2 + t, 0:own]
-        return exchange(here, here, (f, h, s), rows.at[line * 2 + s, 0:own])
+        here = rows.at[line * 2 + t, 0:flat]
+        return exchange(here, here, (f, h, s), rows.at[line * 2 + s, 0:flat])
 
     class Spread:
         def __init__(self, rows):
@@ -576,48 +579,50 @@
             for move in self.down + self.up + self.far + self.near:
                 move.sent()
 
+    grad_spread = Spread(rows_grad)
+
     for b in range(images):
         unit, _ = normal_parts(image(tokens, b))
         normed[b * ROWS : (b + 1) * ROWS, :] = (unit * gain[0:1] + bias[0:1]).astype(BF16)
 
     for step in first:
         step.arrived()
-    grad_spread = Spread(rows_grad)
-    second = [
-        exchange(*[wbuf.at[:, :, t, :, whole(f, 128)]] * 2, (fx[d], h, t),
-                 wbuf.at[:, :, t, :, whole(fx[d], 128)])
-        for d in range(1, 4)
-    ]
+
+    def across_plane(span_i, source, to, landing):
+        here = wbuf.at[span_i, :, t, :, whole(source, 128)]
+        return exchange(here, here, (to, h, t), wbuf.at[span_i, :, t, :, whole(landing, 128)])
+
+    both = [slice(0, 2), slice(2, 4)]
+    second = [across_plane(slice(0, 4), f, fx[d], fx[d]) for d in (1, 2)]
 
     relative = named_in[...] - h * local_count
     wanted = (slots_in[...] >= 0) & (relative >= 0) & (relative < local_count)
     wanted = wanted & (lax.rem(relative + 2 * local_count, 2) == t)
     places = jnp.where(wanted, lax.div(relative, 2) * CAP + slots_in[...], -1)
-    reach = -(-(images * ROWS) // 128) * 128 + 128
+    reach = -(-flat // 128) * 128 + 128
     tail = jnp.full((2, reach), -1, jnp.int32)
     places = jnp.concatenate([places, tail], axis=1)[:, 0 : places.shape[1] // 128 * 128 + reach]
     place_lane = lax.broadcasted_iota(jnp.int32, (2, reach), 1)
     for b in range(2 * H):
-        rows = jnp.full((2, reach), -1, jnp.int32)
-        for i in range(images):
-            begin = (b * images + i) * SEQ - i * ROWS
-            base = max(begin // 128, 0) * 128
-            window = pltpu.roll(places[:, base : base + reach], (base - begin) % reach, 1)
-            inside = (place_lane >= i * ROWS) & (place_lane < i * ROWS + SEQ)
-            rows = jnp.where(inside, window, rows)
+        begin = b * own_rows
+        base = begin // 128 * 128
+        window = pltpu.roll(places[:, base : base + reach], (base - begin) % reach, 1)
+        rows = jnp.where(place_lane < own_rows, window, -1)
         prow[b, 0:2, :] = rows[:, 0 : prow.shape[2]]
 
     def mark_slots(b):
         for part in range(4):
-            spot = lax.broadcasted_iota(jnp.int32, (CAP, own), 0) + CAP * part
-            named = (prow[b, 0:1, 0:own] == spot) | (prow[b, 1:2, 0:own] == spot)
-            big[b, part * CAP : (part + 1) * CAP, 0:own] = jnp.where(named, 1.0, 0.0).astype(BF16)
+            spot = lax.broadcasted_iota(jnp.int32, (CAP, flat), 0) + CAP * part
+            named = (prow[b, 0:1, 0:flat] == spot) | (prow[b, 1:2, 0:flat] == spot)
+            big[b, part * CAP : (part + 1) * CAP, 0:flat] = jnp.where(named, 1.0, 0.0).astype(BF16)
 
     grad_spread.second()
-    pl.loop(0, H)(mark_slots)
+    pl.loop(0, 2 * H)(mark_slots)
+    for d in (1, 2):
+        second[d - 1].arrived()
+        second.append(across_plane(both[d - 1], fx[d], fx[3 - d], fx[3]))
     grad_spread.relay()
-    pl.loop(H, 2 * H)(mark_slots)
-    for step in second:
+    for step in second[2:]:
         step.arrived()
     third = exchange(*[wbuf.at[:, :, t]] * 2, (f, h, s), wbuf.at[:, :, s])
 
@@ -663,7 +668,9 @@
         value = image(tokens, b) + mm(mixed[rows, :], wbuf[3].reshape(width, width))
         middle[rows, :] = value
         unit, _ = normal_parts(value)
-        rows_norm[h * 2 + t, rows, :] = (unit * gain[1:2] + bias[1:2]).astype(BF16)
+        own_sum[0, b * SEQ : (b + 1) * SEQ, :] = (unit * gain[1:2] + bias[1:2])[0:SEQ]
+    own_flat = jnp.where(flat_index < own_rows, own_sum[0, 0:flat, :], 0.0)
+    rows_norm[h * 2 + t, 0:flat, :] = own_flat.astype(BF16)
 
     norm_spread = Spread(rows_norm)
     grad_spread.close()
@@ -671,7 +678,7 @@
     def accumulate(rows, b, begin):
         for part in range(4):
             span_rows = slice(part * CAP, (part + 1) * CAP)
-            value = mm(big[b, span_rows, 0:own], rows[b, 0:own])
+            value = mm(big[b, span_rows, 0:flat], rows[b, 0:flat])
             wide[span_rows, :] = value if begin else wide[span_rows, :] + value
 
     def accumulate_all(spread, order):
@@ -720,13 +727,23 @@
         if d:
             norm_moved[d].arrived()
         rows = xrows[group]
-        result = jnp.zeros((CAP, width), F32)
-        for c in range(chunks):
-            value, slope = gelu_parts(mm(rows, win[:, c * chunk : (c + 1) * chunk]))
+        piece = 256
+        ahead = mm(rows, win[:, 0:piece])
+        result, held = None, None
+        for c in range(win.shape[1] // piece):
+            here_in = slice(c * piece % chunk, c * piece % chunk + piece)
+            hidden = ahead
+            if c + 1 < win.shape[1] // piece:
+                ahead = mm(rows, win[:, (c + 1) * piece : (c + 2) * piece])
+            value, slope = gelu_parts(hidden)
             value = value.astype(BF16)
-            big[c, here, :] = value
-            wide[c * CAP : (c + 1) * CAP, :] = slope
-            result += mm(value, wback[c * chunk : (c + 1) * chunk, :])
+            big[c * piece // chunk, here, here_in] = value
+            wide[c * piece // chunk * CAP : (c * piece // chunk + 1) * CAP, here_in] = slope
+            if c:
+                term = mm(held, wback[(c - 1) * piece : c * piece, :])
+                result = term if c == 1 else result + term
+            held = value
+        result = result + mm(held, wback[win.shape[1] - piece :, :])
         logits = mm(rows, wr[...], NT)
         odds = jnp.exp(logits - jnp.max(logits, axis=-1, keepdims=True))
         odds = odds / jnp.sum(odds, axis=-1, keepdims=True)
@@ -758,14 +775,32 @@
     grad_spread.sent()
     norm_spread.sent()
     flat_rows = xrows[...].reshape(4 * CAP, width)
+    route = mm(logit_grad[...], flat_rows, TN)
+    share_rows = wr.shape[0] // 8
+    for j in range(8):
+        for part in range(2):
+            route_out[j, part * share_rows : (part + 1) * share_rows, :] = route[
+                j * share_rows : (j + 1) * share_rows, part * (width // 2) : (part + 1) * (width // 2)
+            ]
+    route_in[f * 2 + t] = route_out[f * 2 + t]
+    plane_peers = [(d, c) for d in range(4) for c in ((t, s) if d else (s,))]
+    route_moves = [
+        exchange(route_out.at[fx[d] * 2 + c], route_in.at[f * 2 + t], (fx[d], h, c), route_in.at[fx[d] * 2 + c])
+        for d, c in plane_peers
+    ]
     flat_grad = grows[...].reshape(4 * CAP, width)
     for c in range(chunks):
         rows_grad[c] = mm(flat_rows, big[4 + c], TN).astype(BF16)
         rows_norm[c] = mm(big[c], flat_grad, TN).astype(BF16)
-    route = mm(logit_grad[...], flat_rows, TN)
-    share_rows = wr.shape[0] // 8
-    for j in range(8):
-        route_out[j, 0:share_rows, :] = route[j * share_rows : (j + 1) * share_rows]
+    for move in route_moves:
+        move.arrived()
+    route = route_in[0]
+    for j in range(1, 8):
+        route = route + route_in[j]
+    route_z[h] = route
+    route_line = [
+        exchange(route_z.at[h], route_z.at[h], (f, hz[d], t), route_z.at[hfrom[d]]) for d in range(1, H)
+    ]
 
     for move in back_moves:
         move.arrived()
@@ -794,16 +829,9 @@
             for c in (t, s):
                 to_owner(d, c, part, back)
 
-    plane_peers = [(d, c) for d in range(4) for c in ((t, s) if d else (s,))]
-    route_in[f * 2 + t] = route_out[f * 2 + t]
-    route_moves = [
-        exchange(route_out.at[fx[d] * 2 + c], route_in.at[f * 2 + t], (fx[d], h, c), route_in.at[fx[d] * 2 + c])
-        for d, c in plane_peers
-    ]
-
     def share(b, back):
-        spots = jnp.transpose(prow[b])[0:own]
-        slot = lax.broadcasted_iota(jnp.int32, (own, 4 * CAP), 1)
+        spots = jnp.transpose(prow[b])[0:flat]
+        slot = lax.broadcasted_iota(jnp.int32, (flat, 4 * CAP), 1)
         named = (spots[:, 0:1] == slot) | (spots[:, 1:2] == slot)
         return mm(jnp.where(named, 1.0, 0.0).astype(BF16), back[...].reshape(4 * CAP, width))
 
@@ -825,7 +853,7 @@
             self.near[place].arrived()
             value = value + sib_in[self.which, place].astype(F32)
             if place == 3:
-                own_sum[self.which] = value
+                own_sum[self.which, 0:flat, :] = value
             else:
                 self.far_out(place)[...] = value.astype(BF16)
 
@@ -848,18 +876,13 @@
                 rows[...] = (rows[...].astype(F32) + passed).astype(BF16)
                 self.last.append(self.hop(place, part, to, place))
 
-        def total(self, rows):
+        def total(self):
             for move in self.last:
                 move.arrived()
-            total = own_sum[self.which, rows, :]
+            total = own_sum[self.which, 0:flat, :]
             for slot in (1, 2):
-                total = total + z_in[self.which, slot, rows, :].astype(F32)
-            return total
-
-    def to_owners_first():
-        to_owners(0, True)
-        to_owners(1, True)
-        to_owners(0, False)
+                total = total + z_in[self.which, slot].astype(F32)
+            own_sum[self.which, 0:flat, :] = total
 
     norm_sums = Gather(0, xback, lambda place: sib_out.at[place], lambda place: z_out.at[place])
     norm_sums.give(0)
@@ -875,9 +898,11 @@
     norm_sums.take(3)
     for move in out_moves:
         move.arrived()
-    to_owners_first()
+    to_owners(0, True)
+    to_owners(1, True)
+    to_owners(0, False)
     out_sums = Gather(
-        1, gback, lambda place: big.at[place, 0:own], lambda place: big.at[4 + place, 0:own]
+        1, gback, lambda place: big.at[place, 0:flat], lambda place: big.at[4 + place, 0:flat]
     )
     out_sums.give(0)
     out_sums.take(0)
@@ -887,23 +912,13 @@
     for place in range(1, 4):
         out_sums.take(place)
 
-    for move in route_moves:
-        move.arrived()
-    route = route_in[0, 0:share_rows, :]
-    for j in range(1, 8):
-        route = route + route_in[j, 0:share_rows, :]
-    route_z[h, 0:share_rows, :] = route
-    route_line = [
-        exchange(route_z.at[h], route_z.at[h], (f, hz[d], t), route_z.at[hfrom[d]]) for d in range(1, H)
-    ]
-
-    for move in norm_sums.last:
-        move.arrived()
+
+    norm_sums.total()
     out_sums.start()
     small_c[t] = jnp.zeros(small_c.shape[1:], F32)
     for b in range(images):
         rows = slice(b * ROWS, (b + 1) * ROWS)
-        grad = norm_sums.total(rows)
+        grad = jnp.where(row_index < SEQ, own_sum[0, b * SEQ : b * SEQ + ROWS, :], 0.0)
         unit, scale = normal_parts(middle[rows, :])
         small_c[t, 1:2] += jnp.sum(grad * unit, axis=0, keepdims=True)
         small_c[t, 3:4] += jnp.sum(grad, axis=0, keepdims=True)
@@ -1045,13 +1060,15 @@
     for move in route_last:
         move.arrived()
     for j in range(8):
-        wrg[j * share_rows : (j + 1) * share_rows, :] = route_all[j, 0:share_rows, :]
-
+        for part in range(2):
+            wrg[j * share_rows : (j + 1) * share_rows, part * (width // 2) : (part + 1) * (width // 2)] = (
+                route_all[j, part * share_rows : (part + 1) * share_rows, :]
+            )
+
+    out_sums.total()
     for b in range(images):
-        rows = slice(b * ROWS, (b + 1) * ROWS)
-        value = middle[rows, :] + out_sums.total(rows)
-        stage[b * SEQ : (b + 1) * SEQ, :] = value[0:SEQ]
-    out[...] = stage[0 : images * SEQ, :].astype(BF16)
+        stage[b * SEQ : (b + 1) * SEQ, :] = middle[b * ROWS : b * ROWS + SEQ, :]
+    out[...] = (stage[0:own_rows, :] + own_sum[1, 0:own_rows, :]).astype(BF16)
 
     for move in line:
         move.arrived()
@@ -1121,6 +1138,7 @@
     own_rows, width = tokens.shape
     images = own_rows // SEQ
     own = images * ROWS
+    flat = -(-own_rows // 16) * 16
     local_count, depth, span = w_in.shape[1:]
     experts = w_router.shape[2]
     hidden = span * 2
@@ -1152,7 +1170,7 @@
         out_specs=[vmem] * 7 + [anywhere] * 2,
         scratch_shapes=[
             full(images * SEQ + 16, width),
-            pltpu.VMEM((2 * H, 8, -(-own // 128) * 128), jnp.int32),
+            pltpu.VMEM((2 * H, 8, -(-flat // 128) * 128), jnp.int32),
             low(4, H, 2, 64, width),
             low(width, hidden),
             low(hidden, width),
@@ -1173,10 +1191,10 @@
             full(own, width),
             full(own, width),
             low(4 * CAP, experts),
-            low(H, own, width),
-            low(2, H, own, width),
-            low(3, own, width),
-            low(2, 3, own, width),
+            low(H, flat, width),
+            low(2, H, flat, width),
+            low(3, flat, width),
+            low(2, 3, flat, width),
             full(2, own, width),
             low(4, H * 64, width),
             low(4, 4, H * 64, 128),
@@ -1185,10 +1203,10 @@
             full(2, 8, width),
             full(4, 8, width),
             full(H, 8, width),
-            full(8, 8, width),
-            full(8, 8, width),
-            full(H, 8, width),
-            full(8, 8, width),
+            full(8, experts // 4, width // 2),
+            full(8, experts // 4, width // 2),
+            full(H, experts // 4, width // 2),
+            full(8, experts // 4, width // 2),
             pltpu.SemaphoreType.DMA((192,)),
             pltpu.SemaphoreType.DMA((192,)),
             pltpu.SemaphoreType.DMA((16,)),

time: 191 us -> 189 us (0.990)
  Pallas kernels: 187 us -> 184 us
    pallas_call x1, Pallas kernels: 181 us -> 179 us  [fast_device(): pl.pallas_call(lambda *refs: block_kernel(H, images, local_count, refs),...]
where the time goes in v1:
time: 189 us; the launch traced here: 186 us
  Pallas kernels  184 us (97%)
    pallas_call x1, Pallas kernels, fast_device(): pl.pallas_call(lambda *refs: block_kernel(H, images, local_count, refs),...  179 us
    pallas_call x1, Pallas kernels, fast_device(): pl.pallas_call(finish_kernel, out_shape=[shape(part.shape, F32 if i >= 7...  5.41 us

profile of v1, /device:TPU:0, one launch (start us, length us, event | category | flops | bytes accessed | tf_op | source)
XLA Modules:
  0.0 185.6 jit_solution(11886871393546777914)
XLA Ops:
  1.3 178.7 %block.1 = (bf16[394,512]{1,0:T(8,128)(2,1)}, f32[394,512]{1,0:T(8,128)}, f32[3,64,128]{2,1,0:T(8,128)}, f32[64,128]{1,0:T(8,128)}, f32[2,512]{1,0:T(2,128)}, /*...) custom-call(bf16[394,512]{1,0:T(8,128)(2,1)} %refs_0_.1, ...), custom_call_target="tpu_custom_call" | custom-call | tf_op jit(solution)/shard_map/block/pallas_call | solution.py:1156
  180.0 5.4 %finish.1 = (bf16[394,512]{1,0:T(8,128)(2,1)}, f32[394,512]{1,0:T(8,128)}, f32[3,64,128]{2,1,0:T(8,128)}, f32[64,128]{1,0:T(8,128)}, f32[2,512]{1,0:T(2,128)}, /...) custom-call(bf16[394,512]{1,0:T(8,128)(2,1)} %get-tuple-element.27.refs_0_, ...), custom_call_target="tpu_custom_call" | custom-call | tf_op jit(solution)/shard_map/finish/pallas_call | solution.py:1224

commit v2 on v1

--- a/solution.py
+++ b/solution.py
@@ -444,7 +444,7 @@
     (
         tokens, cot, counts, wq, wo, gain, bias, wr, win_hbm, wback_hbm, named_in, slots_in,
         out, tgrad, wqg, wog, lng, lnb, wrg, gin_out, gback_out,
-        stage, prow, wbuf, win, wback, rows_grad, rows_norm, big, wide,
+        tgrad_held, stage, prow, wbuf, win, wback, rows_grad, rows_norm, big, wide,
         xsend, gsend, xrows, grows, xback, gback,
         normed, qkv, probs, mixed, middle, grad_mid, logit_grad,
         sib_out, sib_in, z_out, z_in, own_sum,
@@ -770,6 +770,7 @@
             back_moves.append(to_group(d, xsend, xback))
         else:
             xback[f] = total.astype(BF16)
+        if d == 0:
             norm_moved.append(to_group(3, xsend, xrows))
 
     grad_spread.sent()
@@ -888,6 +889,7 @@
     norm_sums.give(0)
     norm_sums.take(0)
     norm_sums.start()
+    to_owners(0, True)
     norm_sums.give(1)
     norm_sums.give(2)
     norm_sums.take(1)
@@ -898,7 +900,6 @@
     norm_sums.take(3)
     for move in out_moves:
         move.arrived()
-    to_owners(0, True)
     to_owners(1, True)
     to_owners(0, False)
     out_sums = Gather(
@@ -1015,7 +1016,8 @@
         small_c[t, 0:1] += jnp.sum(grad * unit, axis=0, keepdims=True)
         small_c[t, 2:3] += jnp.sum(grad, axis=0, keepdims=True)
         grad = normal_pull(grad, unit, scale, gain[0:1]) + grad_mid[rows, :]
-        tgrad[b * SEQ : (b + 1) * SEQ, :] = grad[0:SEQ]
+        tgrad_held[b * SEQ : (b + 1) * SEQ, :] = grad[0:SEQ]
+    kept(tgrad_held, tgrad)
     small_near = exchange(small_c.at[t], small_c.at[t], (f, h, s), small_c.at[s])
 
     planes.append(plane_sums(range(3), [order[3]], nears[3]))
@@ -1037,6 +1039,7 @@
 
     for move in last_plane:
         move.arrived()
+    to_owners(1, False)
     line = []
     for turn in range(3):
         for move in planes[turn]:
@@ -1050,7 +1053,6 @@
         )
     for move in planes[3]:
         move.arrived()
-    to_owners(1, False)
     for move in small_plane:
         move.arrived()
     small_z[h] = (small_p[0] + small_p[1]) + (small_p[2] + small_p[3])
@@ -1167,8 +1169,9 @@
             shape((local_count, span, depth), BF16),
         ),
         in_specs=[vmem, vmem, smem, vmem, vmem, vmem, vmem, vmem, anywhere, anywhere, vmem, vmem],
-        out_specs=[vmem] * 7 + [anywhere] * 2,
+        out_specs=[vmem, anywhere] + [vmem] * 5 + [anywhere] * 2,
         scratch_shapes=[
+            full(own_rows, width),
             full(images * SEQ + 16, width),
             pltpu.VMEM((2 * H, 8, -(-flat // 128) * 128), jnp.int32),
             low(4, H, 2, 64, width),

time: 189 us -> 187 us (0.989)
  no operation moved by 1% of the time
where the time goes in v2:
time: 187 us; the launch traced here: 184 us
  Pallas kernels  183 us (98%)
    pallas_call x1, Pallas kernels, fast_device(): pl.pallas_call(lambda *refs: block_kernel(H, images, local_count, refs),...  177 us
    pallas_call x1, Pallas kernels, fast_device(): pl.pallas_call(finish_kernel, out_shape=[shape(part.shape, F32 if i >= 7...  5.41 us

profile of v2, /device:TPU:0, one launch (start us, length us, event | category | flops | bytes accessed | tf_op | source)
XLA Modules:
  0.0 184.3 jit_solution(13663879009565806266)
XLA Ops:
  1.3 177.4 %block.1 = (bf16[394,512]{1,0:T(8,128)(2,1)}, f32[394,512]{1,0:T(8,128)}, f32[3,64,128]{2,1,0:T(8,128)}, f32[64,128]{1,0:T(8,128)}, f32[2,512]{1,0:T(2,128)}, /*...) custom-call(bf16[394,512]{1,0:T(8,128)(2,1)} %refs_0_.1, ...), custom_call_target="tpu_custom_call" | custom-call | tf_op jit(solution)/shard_map/block/pallas_call | solution.py:1158
  178.7 5.4 %finish.1 = (bf16[394,512]{1,0:T(8,128)(2,1)}, f32[394,512]{1,0:T(8,128)}, f32[3,64,128]{2,1,0:T(8,128)}, f32[64,128]{1,0:T(8,128)}, f32[2,512]{1,0:T(2,128)}, /...) custom-call(bf16[394,512]{1,0:T(8,128)(2,1)} %get-tuple-element.27.refs_0_, ...), custom_call_target="tpu_custom_call" | custom-call | tf_op jit(solution)/shard_map/finish/pallas_call | solution.py:1227

commit v3 on v2

--- a/solution.py
+++ b/solution.py
@@ -510,7 +510,7 @@
         target = wback.at[whole(t, span), whole(f, depth)]
         return exchange(wback_hbm.at[fx[d] * 2 + c], target, (fx[d], h, c), landing)
 
-    expert_moves = [move_in(d, c) for d, c in ((1, t), (2, t), (1, s), (2, s))]
+    expert_moves = [move_in(d, c) for d, c in ((1, t), (2, t))]
     mine = [
         kept(win_hbm.at[f * 2 + t], win.at[whole(f, depth), whole(t, span)]),
         kept(wback_hbm.at[f * 2 + t], wback.at[whole(t, span), whole(f, depth)]),
@@ -626,7 +626,7 @@
         step.arrived()
     third = exchange(*[wbuf.at[:, :, t]] * 2, (f, h, s), wbuf.at[:, :, s])
 
-    for d, c in ((3, t), (3, s), (0, s)):
+    for d, c in ((1, s), (2, s), (3, t), (3, s), (0, s)):
         expert_moves.append(move_in(d, c))
     for d, c in ((1, t), (2, t), (1, s), (2, s), (3, t), (3, s), (0, s)):
         expert_moves.append(move_back(d, c))
@@ -1021,6 +1021,21 @@
     small_near = exchange(small_c.at[t], small_c.at[t], (f, h, s), small_c.at[s])
 
     planes.append(plane_sums(range(3), [order[3]], nears[3]))
+    for move in last_plane:
+        move.arrived()
+    line = []
+
+    def send_line(turn):
+        for move in planes[turn]:
+            move.arrived()
+        other = order[turn]
+        for i in range(4):
+            line_out[other, i] = own_columns(i, other).astype(BF16)
+        landing = line_in.at[hfrom[turn + 1]]
+        line.append(exchange(line_out.at[other], line_in.at[h], (f, other, t), landing))
+
+    send_line(0)
+    send_line(1)
     small_near.arrived()
     small_p[f] = small_c[0] + small_c[1]
     small_plane = [
@@ -1037,20 +1052,8 @@
         for d, c in plane_peers
     ]
 
-    for move in last_plane:
-        move.arrived()
+    send_line(2)
     to_owners(1, False)
-    line = []
-    for turn in range(3):
-        for move in planes[turn]:
-            move.arrived()
-        other = order[turn]
-        for i in range(4):
-            line_out[other, i] = own_columns(i, other).astype(BF16)
-        d = turn + 1
-        line.append(
-            exchange(line_out.at[other], line_in.at[h], (f, other, t), line_in.at[hfrom[d]])
-        )
     for move in planes[3]:
         move.arrived()
     for move in small_plane:

time: 187 us -> 187 us (level)
  no operation moved by 1% of the time
where the time goes in v3:
time: 187 us; the launch traced here: 184 us
  Pallas kernels  183 us (98%)
    pallas_call x1, Pallas kernels, fast_device(): pl.pallas_call(lambda *refs: block_kernel(H, images, local_count, refs),...  177 us
    pallas_call x1, Pallas kernels, fast_device(): pl.pallas_call(finish_kernel, out_shape=[shape(part.shape, F32 if i >= 7...  5.41 us

profile of v3, /device:TPU:0, one launch (start us, length us, event | category | flops | bytes accessed | tf_op | source)
XLA Modules:
  0.0 184.2 jit_solution(13963589800829856771)
XLA Ops:
  1.3 177.3 %block.1 = (bf16[394,512]{1,0:T(8,128)(2,1)}, f32[394,512]{1,0:T(8,128)}, f32[3,64,128]{2,1,0:T(8,128)}, f32[64,128]{1,0:T(8,128)}, f32[2,512]{1,0:T(2,128)}, /*...) custom-call(bf16[394,512]{1,0:T(8,128)(2,1)} %refs_0_.1, ...), custom_call_target="tpu_custom_call" | custom-call | tf_op jit(solution)/shard_map/block/pallas_call | solution.py:1161
  178.6 5.4 %finish.1 = (bf16[394,512]{1,0:T(8,128)(2,1)}, f32[394,512]{1,0:T(8,128)}, f32[3,64,128]{2,1,0:T(8,128)}, f32[64,128]{1,0:T(8,128)}, f32[2,512]{1,0:T(2,128)}, /...) custom-call(bf16[394,512]{1,0:T(8,128)(2,1)} %get-tuple-element.27.refs_0_, ...), custom_call_target="tpu_custom_call" | custom-call | tf_op jit(solution)/shard_map/finish/pallas_call | solution.py:1230
